TPU v7x, 32 devices: a whole 2x2x4 slice. The times are simulated.
32 devices in a mesh: visit: 8 (over z, core), patch: 4 (over y, x).
Axes of the slice: x: 2, y: 2, z: 4, core: 2. Of those that a mesh axis runs over, the one named last changes fastest.
Arguments:
- images: bfloat16 [8, 1024, 4096], P('visit', 'patch'), may hold values from -6 to 6
- psf_taps: bfloat16 [8, 2, 13], P('visit'), may hold values from 0.019897461 to 0.19921875
- exposure_weights: float32 [8], P('visit'), may hold values from 0.5 to 8
- dest_patch: int32 [8, 8, 32], P('visit', 'patch'), may hold values from -1 to 3, as said below
- dest_cell: int32 [8, 8, 32], P('visit', 'patch'), may hold values from -1 to 63, as said below
- shift_class: int32 [8, 2, 8, 32], P('visit', None, 'patch'), may hold values from 0 to 7
Outputs:
- coadd: float32 [4, 64, 128, 128], P('patch', 'visit')
- weight_map: float32 [4, 64], P('patch', 'visit')
Inputs may be any that keep to these rules, and one draw needn't show every extreme that they name: `dest_patch`: within one exposure all tiles move to sky cells by one whole-cell offset of at most 2 cells along each direction, so distinct tiles land in distinct cells; the patch of cell row u and column w is (u // 8) * 4 + w // 8. Of the 64 tiles in one exposure's band of 256 rows, at most 16 fall in any one patch. `dest_cell`: cell index (u % 8) * 8 + w % 8; -1 exactly where dest_patch is -1.
All inputs are finite; a program needn't handle non-finite values.
Results may differ from a plain program's by a relative error of at most 0.0004.
The roundings to bfloat16 on the way count: a program that leaves them out, or rounds other values in their place, can miss the bound.
Values may be sent and summed in bfloat16 or wider, within the bound.
A program may use at most 128 MiB of HBM per device.

v0:
```python
import jax
import jax.numpy as jnp
from jax import lax
from jax.sharding import PartitionSpec as P

TILE = 128
KTAPS = 13
SHIFTS = 8
CELLS = 64
CAP = 16


def padded_2(cells, sides, width):
    for axis, dim in sides:
        count = lax.axis_size(axis)
        ends = count - 1
        head = lax.slice_in_dim(cells, 0, width, axis=dim)
        tail = lax.slice_in_dim(cells, cells.shape[dim] - width, cells.shape[dim], axis=dim)
        cells = jnp.concatenate(
            [
                lax.ppermute(tail, axis, [(i, (i + 1) % count) for i in range(ends)]),
                cells,
                lax.ppermute(head, axis, [((i + 1) % count, i) for i in range(ends)]),
            ],
            axis=dim,
        )
    return cells


def passed_along(x, axis, by):
    size = lax.axis_size(axis)
    pairs = [(i, i + by) for i in range(size) if 0 <= i + by < size]
    return lax.ppermute(x, axis, pairs)


def lanczos_table(size, classes):
    out_pos = jnp.arange(size, dtype=jnp.float32)[None, :, None]
    src_pos = jnp.arange(size + 6, dtype=jnp.float32)[None, None, :] - 3.0
    frac = jnp.arange(classes, dtype=jnp.float32)[:, None, None] / classes
    dist = src_pos - out_pos - frac
    kernel = jnp.where(jnp.abs(dist) < 3.0, jnp.sinc(dist) * jnp.sinc(dist / 3.0), 0.0)
    kernel = kernel / jnp.sum(kernel, axis=2, keepdims=True)
    return kernel.astype(jnp.bfloat16)


def column_pass(rows, taps):
    count, height, cols = rows.shape
    reach = KTAPS // 2
    blocks = cols // TILE
    padded = jnp.pad(rows, ((0, 0), (0, 0), (reach, TILE - reach)))
    main = padded[:, :, :cols].reshape(count, height, blocks, TILE)
    tail = padded[:, :, TILE : TILE + cols].reshape(count, height, blocks, TILE)[..., : 2 * reach]
    windows = jnp.concatenate([main, tail], axis=3)
    offset = jnp.arange(TILE + 2 * reach)[:, None] - jnp.arange(TILE)[None, :]
    marks = (offset[None] == jnp.arange(KTAPS)[:, None, None]).astype(jnp.float32)
    toeplitz = jnp.einsum("eb,bji->eji", taps.astype(jnp.float32), marks).astype(jnp.bfloat16)
    result = jnp.einsum("enxj,eji->enxi", windows, toeplitz, preferred_element_type=jnp.float32)
    return result.reshape(count, height, cols).astype(jnp.bfloat16)


def row_pass(colpassed, taps, out_rows):
    offset = jnp.arange(out_rows + KTAPS - 1)[None, :] - jnp.arange(out_rows)[:, None]
    marks = (offset[None] == jnp.arange(KTAPS)[:, None, None]).astype(jnp.float32)
    toeplitz = jnp.einsum("eb,bor->eor", taps.astype(jnp.float32), marks).astype(jnp.bfloat16)
    return jnp.einsum("eor,erc->eoc", toeplitz, colpassed, preferred_element_type=jnp.float32)


def tile_windows(framed):
    count, height, cols = framed.shape
    band = height - 6
    padded = jnp.pad(framed, ((0, 0), (0, TILE - 6), (3, TILE - 3)))
    count_y = band // TILE
    count_x = cols // TILE
    width = cols + TILE
    rmain = padded[:, :band].reshape(count, count_y, TILE, width)
    rtail = padded[:, TILE : TILE + band].reshape(count, count_y, TILE, width)[:, :, :6]
    rowwin = jnp.concatenate([rmain, rtail], axis=2)
    cmain = rowwin[..., :cols].reshape(count, count_y, TILE + 6, count_x, TILE)
    ctail = rowwin[..., TILE : TILE + cols].reshape(count, count_y, TILE + 6, count_x, TILE)[
        ..., :6
    ]
    return jnp.concatenate([cmain, ctail], axis=4)


def pick_table(classes, table):
    marks = (classes[..., None] == jnp.arange(SHIFTS, dtype=classes.dtype)).astype(jnp.bfloat16)
    flat = table.reshape(SHIFTS, -1)
    chosen = jnp.dot(marks.reshape(-1, SHIFTS), flat, preferred_element_type=jnp.float32)
    return chosen.astype(jnp.bfloat16).reshape(classes.shape + table.shape[1:])


def local(images, psf_taps, exposure_weights, dest_patch, dest_cell, shift_class):
    count = images.shape[0]
    band = images.shape[1]
    cols = images.shape[2]
    owners = lax.axis_size("patch")
    table = lanczos_table(TILE, SHIFTS)
    reach = KTAPS // 2
    raw = padded_2(images, (("patch", 1),), reach)
    colpassed = column_pass(raw, psf_taps[:, 1])
    matched = row_pass(colpassed, psf_taps[:, 0], band).astype(jnp.bfloat16)
    framed = padded_2(matched, (("patch", 1),), 3)
    tiles = tile_windows(framed)
    along_cols = pick_table(shift_class[:, 1], table)
    half = jnp.einsum(
        "eyrxj,eyxij->eyxri", tiles, along_cols, preferred_element_type=jnp.float32
    ).astype(jnp.bfloat16)
    count_y = band // TILE
    count_x = cols // TILE
    per_expo = count_y * count_x
    patch_flat = dest_patch.reshape(count, per_expo)
    hits = (patch_flat[..., None] == jnp.arange(owners, dtype=jnp.int32)).astype(jnp.int32)
    rank = jnp.sum(jnp.cumsum(hits, axis=1) * hits, axis=2) - 1
    expo_index = jnp.arange(count, dtype=jnp.int32)[:, None]
    cell_values = dest_cell.reshape(count, per_expo).astype(jnp.float32) + 1.0
    along_rows = pick_table(shift_class[:, 0], table)
    warped = jnp.einsum(
        "eyxor,eyxri->eyxoi", along_rows, half, preferred_element_type=jnp.float32
    ).astype(jnp.bfloat16)
    content = warped.reshape((count * per_expo, TILE, TILE))
    extra = cell_values[..., None]
    width = extra.shape[-1]
    extra = extra.reshape(count * per_expo, width)
    item_shape = content.shape[1:]
    flat_content = content.reshape(count * per_expo, -1)
    cell_numbers = (jnp.arange(CELLS) + 1).astype(jnp.bfloat16)
    state = (jnp.zeros((CELLS, TILE * TILE), jnp.float32), jnp.zeros((CELLS,), jnp.float32))
    position = lax.axis_index("patch")
    span = min(4, owners - 1)
    for offset in range(-span, span + 1):
        slot = jnp.where(
            patch_flat == position + offset, expo_index * CAP + rank, count * CAP
        ).reshape(-1)
        slots = count * CAP
        picks = jnp.arange(slots, dtype=jnp.int32)[:, None] == slot[None, :]
        pack_placed = jnp.dot(
            picks.astype(jnp.bfloat16), flat_content, preferred_element_type=jnp.float32
        )
        pack_buffer = pack_placed.astype(jnp.bfloat16).reshape((slots,) + item_shape)
        pack_labels = jnp.dot(
            picks.astype(jnp.float32), extra, precision=lax.Precision.HIGHEST
        ).astype(jnp.bfloat16)
        buffer = pack_buffer
        labels = pack_labels
        buffer = buffer.reshape((1, count, CAP) + item_shape)
        labels = labels.reshape(1, count, CAP, width)
        if offset != 0:
            buffer, labels = passed_along((buffer, labels), "patch", offset)
        accumulate_total, accumulate_cover = state
        chosen = (cell_numbers[:, None] == labels[:, 0, :, 0]).astype(jnp.bfloat16)
        placed = jnp.dot(
            chosen, buffer[:, 0].reshape(-1, TILE * TILE), preferred_element_type=jnp.float32
        )
        accumulate_total = accumulate_total + exposure_weights[0] * placed
        accumulate_cover = accumulate_cover + exposure_weights[0] * jnp.sum(
            chosen.astype(jnp.float32), axis=1
        )
        state = (accumulate_total, accumulate_cover)
    total, cover = state
    total_sum, cover_sum = (
        lax.psum_scatter(
            total.reshape(1, CELLS, TILE, TILE), "visit", scatter_dimension=1, tiled=True
        ),
        lax.psum_scatter(cover.reshape(1, CELLS), "visit", scatter_dimension=1, tiled=True),
    )
    coadd = total_sum / jnp.maximum(cover_sum, 1.0)[:, :, None, None]
    return (coadd, cover_sum)


def solution(mesh):
    placed = (
        P("visit", "patch", None),
        P("visit", None, None),
        P("visit"),
        P("visit", "patch", None),
        P("visit", "patch", None),
        P("visit", None, "patch", None),
    )
    return jax.shard_map(
        local,
        mesh=mesh,
        in_specs=placed,
        out_specs=(P("patch", "visit", None, None), P("patch", "visit")),
        check_vma=False,
    )
```

profile of v0, /device:TPU:0, one launch (start us, length us, event | category | flops | bytes accessed | tf_op | source)
XLA Modules:
  0.0 235.5 jit_solution(15150598637762663547)
XLA Ops:
  7.2 0.9 fusion.198
  8.1 4.8 %collective-permute-start.1 = (bf16[1,6,4096]{2,1,0:T(8,128)(2,1)S(1)}, bf16[1,6,4096]{2,1,0:T(8,128)(2,1)S(1)}, u32[]{:S(2)}, u32[]{:S(2)}) collective-permute-start(bf16[1,6,4096]{2,1,0:T(8,128)(2,1)S(1)} %get-tuple-element.20), channel_id=1, source_target_pairs={{0,1},{1,2},{2,3},{4,5},{5,6},{6,7},{8,9},{9,10},{10,11},{12,13},{... | collective-permute-start | bytes 147464 | tf_op jit(solution)/shard_map/ppermute | solution.py:21
  13.0 1.3 collective-permute-start.2
  14.3 0.8 reshape.480
  15.4 0.7 convert_add_fusion
  16.3 1.3 collective-permute-start.8
  17.7 1.3 collective-permute-start.6
  19.1 1.3 collective-permute-start
  21.5 1.0 fusion.18
  22.5 3.0 %fusion.150 = f32[8,128]{1,0:T(8,128)S(1)} fusion(f32[8]{0:T(128)S(1)} %iota_multiply_fusion, f32[128,134]{1,0:T(8,128)S(1)} %iota_subtract_fusion.1), kind=kLoop, calls=%fused_computation.181 | loop fusion | flops 9878528 | bytes 72736 | tf_op jit(solution)/shard_map/reduce_sum | solution.py:42
  25.5 2.8 %divide_convert_fusion = bf16[8,128,134]{2,1,0:T(8,128)(2,1)S(1)} fusion(f32[8,128]{1,0:T(8,128)S(1)} %fusion.150, f32[8]{0:T(128)S(1)} %iota_multiply_fusion, f32[128,134]{1,0:T(8,128)S(1)} %iota_subtract_fusion.1), kind=kLoop, calls=%fused_computation.156 | loop fusion | flops 10016768 | bytes 347168 | tf_op jit(solution)/shard_map/convert_element_type | solution.py:43
  28.3 0.6 reshape.482
  29.1 0.8 convolution_convert_fusion.1
  29.9 2.2 convolution_convert_fusion
  32.8 3.3 %fusion.34 = bf16[1,268,4224]{2,1,0:T(8,128)(2,1)S(1)} fusion(bf16[1,6,4096]{2,1,0:T(8,128)(2,1)S(1)} %collective-permute-done.2, bf16[1,256,4096]{2,1,0:T(8,128)(2,1)} %param.7, bf16[1,6,4096]{2,1,0:T(8,128)(2,1)S(1)} %collective-permute-done.1), kind=kLoop, calls=%fused_computation.60 | loop fusion | flops 13584384 | bytes 4459520 | tf_op jit(solution)/shard_map/concatenate | solution.py:19
  38.5 1.3 fusion.52
  40.1 1.1 copy.29
  41.2 1.3 fusion.10
  42.5 1.3 copy-done.1
  43.8 4.5 %collective-permute-start.3 = (bf16[1,3,4096]{2,1,0:T(4,128)(2,1)S(1)}, bf16[1,3,4096]{2,1,0:T(4,128)(2,1)S(1)}, u32[]{:S(2)}, u32[]{:S(2)}) collective-permute-start(bf16[1,3,4096]{2,1,0:T(4,128)(2,1)S(1)} %get-tuple-element.18), channel_id=1, source_target_pairs={{0,1},{1,2},{2,3},{4,5},{5,6},{6,7},{8,9},{9,10},{10,11},{12,13},{... | collective-permute-start | bytes 73736 | tf_op jit(solution)/shard_map/ppermute | solution.py:21
  48.4 1.3 collective-permute-start.4
  49.7 13.2 %reshape.483 = bf16[2,32,128,134]{3,2,1,0:T(8,128)(2,1)} reshape(bf16[64,17152]{1,0:T(8,128)(2,1)S(1)} %convolution_convert_fusion.1) | data formatting | bytes 4390912 | tf_op jit(solution)/shard_map/reshape.47
  62.9 14.5 %reshape.494 = bf16[2,32,128,134]{3,2,1,0:T(8,128)(2,1)} reshape(bf16[64,17152]{1,0:T(8,128)(2,1)} %convolution_convert_fusion) | data formatting | bytes 4390912 | tf_op jit(solution)/shard_map/reshape.22
  78.0 8.9 %fusion.22 = bf16[1,384,4224]{2,1,0:T(8,128)(2,1)S(1)} fusion(bf16[1,3,4096]{2,1,0:T(4,128)(2,1)S(1)} %collective-permute-done.4, bf16[1,256,4096]{2,1,0:T(8,128)(2,1)S(1)} %copy-done.2, bf16[1,3,4096]{2,1,0:T(4,128)(2,1)S(1)} %collective-permute-done.3), kind=kLoop, calls=%fused_computation.48 | loop fusion | flops 27574272 | bytes 5390336 | tf_op jit(solution)/shard_map/concatenate | solution.py:19
  87.2 1.7 fusion.38
  89.0 3.4 %reshape.491 = bf16[1,2,134,32,128]{4,3,2,1,0:T(8,128)(2,1)} reshape(bf16[1,2,134,4096]{3,2,1,0:T(8,128)(2,1)} %get-tuple-element.14) | data formatting | bytes 4390912 | tf_op jit(solution)/shard_map/reshape | solution.py:78
  92.4 3.9 %copy.15 = bf16[1,2,134,32,128]{4,2,3,1,0:T(8,128)(2,1)} copy(bf16[1,2,134,32,128]{4,3,2,1,0:T(8,128)(2,1)} %reshape.491) | data formatting | bytes 4390912 | tf_op jit(solution)/shard_map/reshape | solution.py:78
  96.2 2.5 %reshape.492 = bf16[1,2,134,32,128]{4,3,2,1,0:T(8,128)(2,1)} reshape(bf16[1,2,134,4096]{3,2,1,0:T(8,128)(2,1)S(1)} %get-tuple-element.15) | data formatting | bytes 4390912 | tf_op jit(solution)/shard_map/reshape | solution.py:79
  98.8 3.9 %copy.26 = bf16[1,2,134,32,6]{4,2,3,1,0:T(8,128)(2,1)} copy(bf16[1,2,134,32,6]{4,3,2,1,0:T(8,128)(2,1)} %bitcast.237) | data formatting | bytes 205824
  102.6 7.2 %fusion.53 = bf16[2,32,128,128]{3,2,1,0:T(8,128)(2,1)S(1)} fusion(bf16[2,32,128,134]{3,2,1,0:T(8,128)(2,1)} %reshape.483, bf16[2,32,128,134]{3,2,1,0:T(8,128)(2,1)} %reshape.494, bf16[1,2,134,32,6]{4,2,3,1,0:T(8,128)(2,1)} %copy.26, bf16[1,2,134,32,128]{4,2,3,1,0:T(8,128)(2,1)} %copy.15), kind=kOutput, calls=%fused_computation.84 | convolution fusion | flops 581952512 | bytes 8786432 | tf_op jit(solution)/shard_map/eyxor,eyxri->eyxoi/dot_general | solution.py:117
  109.8 1.2 fusion.67
  111.0 1.2 fusion.64
  112.3 1.2 fusion.61
  113.5 1.2 fusion.73
  114.7 1.2 fusion.76
  116.0 0.9 copy.35
  116.9 1.3 collective-permute-start.9
  118.2 0.9 copy.33
  119.1 1.5 collective-permute-start.7
  120.5 0.9 copy.31
  121.4 0.9 copy.39
  122.3 0.9 copy.41
  123.2 3.7 %fusion.59 = f32[64,16384]{1,0:T(8,128)} fusion(bf16[8,8,128,128]{3,2,1,0:T(8,128)(2,1)S(1)} %bitcast.228, s32[64]{0:T(128)S(1)} %get-tuple-element.27, bf16[64]{0:T(256)(128)(2,1)S(1)} %add_convert_fusion, bf16[16]{0:T(256)(128)(2,1)S(1)} %fusion.87), kind=kOutput, calls=%fused_computation.91 | convolution fusion | flops 67373056 | bytes 6291872 | tf_op jit(solution)/shard_map/dot_general | solution.py:151
  127.0 1.2 fusion.70
  128.3 7.5 %collective-permute-start.12 = (bf16[1,1,16,1]{2,3,1,0:T(2,128)(2,1)S(1)}, bf16[1,1,16,1]{2,3,1,0:T(2,128)(2,1)S(1)}, u32[]{:S(2)}, u32[]{:S(2)}) collective-permute-start(bf16[1,1,16,1]{2,3,1,0:T(2,128)(2,1)S(1)} %fusion.91), channel_id=1, source_target_pairs={{0,2},{1,3},{4,6},{5,7},{8,10},{9,11},{12,14},{13,15},{16,18},{17,... | collective-permute-start | bytes 104 | tf_op jit(solution)/shard_map/ppermute | solution.py:33
  135.9 2.3 collective-permute-start.13
  138.2 0.8 fusion.142
  139.0 1.8 collective-permute-start.14
  140.8 7.4 %collective-permute-start.15 = (bf16[1,1,16,128,128]{4,3,2,1,0:T(8,128)(2,1)S(1)}, bf16[1,1,16,128,128]{4,3,2,1,0:T(8,128)(2,1)S(1)}, u32[]{:S(2)}, u32[]{:S(2)}) collective-permute-start(bf16[1,1,16,128,128]{4,3,2,1,0:T(8,128)(2,1)S(1)} %bitcast.248), channel_id=1, source_target_pairs={{0,3},{4,7},{8,11},{12,15},{16,19},{20,23},{24,27},{28,31}} | collective-permute-start | bytes 1572872 | tf_op jit(solution)/shard_map/ppermute | solution.py:33
  148.2 0.8 fusion.145
  149.1 1.6 collective-permute-start.10
  150.7 1.3 collective-permute-start.5
  152.0 0.8 fusion.137
  152.8 1.4 collective-permute-start.11
  154.2 6.3 %collective-permute-done.15 = bf16[1,1,16,128,128]{4,3,2,1,0:T(8,128)(2,1)S(1)} collective-permute-done((bf16[1,1,16,128,128]{4,3,2,1,0:T(8,128)(2,1)S(1)}, bf16[1,1,16,128,128]{4,3,2,1,0:T(8,128)(2,1)S(1)}, u32[]{:S(2)}, u32[]{:S(2)}) %collective-permute-start.15) | collective-permute-done | bytes 524320 | tf_op jit(solution)/shard_map/ppermute | solution.py:33
  160.5 0.8 fusion.134
  161.3 5.7 %collective-permute-done.5 = bf16[1,1,16,128,128]{4,3,2,1,0:T(8,128)(2,1)S(1)} collective-permute-done((bf16[1,1,16,128,128]{4,3,2,1,0:T(8,128)(2,1)S(1)}, bf16[1,1,16,128,128]{4,3,2,1,0:T(8,128)(2,1)S(1)}, u32[]{:S(2)}, u32[]{:S(2)}) %collective-permute-start.5) | collective-permute-done | bytes 524320 | tf_op jit(solution)/shard_map/ppermute | solution.py:33
  167.0 1.2 fusion.3
  168.3 2.5 %collective-permute-done.11 = bf16[1,1,16,128,128]{4,3,2,1,0:T(8,128)(2,1)S(1)} collective-permute-done((bf16[1,1,16,128,128]{4,3,2,1,0:T(8,128)(2,1)S(1)}, bf16[1,1,16,128,128]{4,3,2,1,0:T(8,128)(2,1)S(1)}, u32[]{:S(2)}, u32[]{:S(2)}) %collective-permute-start.11) | collective-permute-done | bytes 524320 | tf_op jit(solution)/shard_map/ppermute | solution.py:33
  170.8 1.3 fusion.41
  172.1 2.7 %copy.43 = f32[8,8,128,128]{3,2,1,0:T(8,128)} copy(f32[8,8,128,128]{3,1,2,0:T(8,128)S(1)} %fusion.41) | data formatting | bytes 8388608
  176.8 16.3 %all-reduce.2 = f32[1,64]{1,0:T(1,128)S(1)} all-reduce(f32[1,64]{1,0:T(1,128)S(1)} %multiply_bitcast_fusion), channel_id=3, replica_groups=mesh['visit'=8,'patch'=4] {'visit'}, use_global_device_ids=true, to_apply=%region_11.13.clone | all-reduce | flops 64 | bytes 512
  193.7 32.8 %reduce-scatter.3.cloned.1.call-done = f32[1,8,128,128]{3,2,1,0:T(8,128)} async-done(((f32[1,64,128,128]{3,2,1,0:T(8,128)}), f32[1,8,128,128]{3,2,1,0:T(8,128)}) %reduce-scatter.3.cloned.1.call-update) | async-done | bytes 524304 | tf_op jit(solution)/shard_map/reduce_scatter | solution.py:161
  226.5 1.9 broadcast_divide_fusion
  (71 shorter events, 7.9 us)
Async XLA Ops:
  7.2 14.0 %copy-start.7 = (bf16[1,2,13]{2,1,0:T(2,128)(2,1)S(1)}, bf16[1,2,13]{2,1,0:T(2,128)(2,1)}, u32[]{:S(2)}) copy-start(bf16[1,2,13]{2,1,0:T(2,128)(2,1)} %param.8) | copy-start | bytes 160
  7.2 219.3 %reduce-scatter.3.cloned.1.call-start = ((), (), s32[]{:S(2)}) async-start(), calls=%async_computation.1 | async-start | bytes 4718592 | tf_op jit(solution)/shard_map/reduce_scatter | solution.py:161
  8.1 24.7 %collective-permute-start.1 = (bf16[1,6,4096]{2,1,0:T(8,128)(2,1)S(1)}, bf16[1,6,4096]{2,1,0:T(8,128)(2,1)S(1)}, u32[]{:S(2)}, u32[]{:S(2)}) collective-permute-start(bf16[1,6,4096]{2,1,0:T(8,128)(2,1)S(1)} %get-tuple-element.20), channel_id=1, source_target_pairs={{0,1},{1,2},{2,3},{4,5},{5,6},{6,7},{8,9},{9,10},{10,11},{12,13},{... | collective-permute-start | bytes 147464 | tf_op jit(solution)/shard_map/ppermute | solution.py:21
  13.0 19.8 %collective-permute-start.2 = (bf16[1,6,4096]{2,1,0:T(8,128)(2,1)S(1)}, bf16[1,6,4096]{2,1,0:T(8,128)(2,1)S(1)}, u32[]{:S(2)}, u32[]{:S(2)}) collective-permute-start(bf16[1,6,4096]{2,1,0:T(8,128)(2,1)S(1)} %get-tuple-element.21), channel_id=1, source_target_pairs={{1,0},{2,1},{3,2},{5,4},{6,5},{7,6},{9,8},{10,9},{11,10},{13,12},{... | collective-permute-start | bytes 147464 | tf_op jit(solution)/shard_map/ppermute | solution.py:23
  16.3 112.0 %collective-permute-start.8 = (bf16[1,1,16,1]{2,3,1,0:T(2,128)(2,1)S(1)}, bf16[1,1,16,1]{2,3,1,0:T(2,128)(2,1)S(1)}, u32[]{:S(2)}, u32[]{:S(2)}) collective-permute-start(bf16[1,1,16,1]{2,3,1,0:T(2,128)(2,1)S(1)} %fusion.86), channel_id=1, source_target_pairs={{1,0},{2,1},{3,2},{5,4},{6,5},{7,6},{9,8},{10,9},{11,10},{13,12},{... | collective-permute-start | bytes 104 | tf_op jit(solution)/shard_map/ppermute | solution.py:33
  17.7 121.3 %collective-permute-start.6 = (bf16[1,1,16,1]{2,3,1,0:T(2,128)(2,1)S(1)}, bf16[1,1,16,1]{2,3,1,0:T(2,128)(2,1)S(1)}, u32[]{:S(2)}, u32[]{:S(2)}) collective-permute-start(bf16[1,1,16,1]{2,3,1,0:T(2,128)(2,1)S(1)} %fusion.84), channel_id=1, source_target_pairs={{2,0},{3,1},{6,4},{7,5},{10,8},{11,9},{14,12},{15,13},{18,16},{19,... | collective-permute-start | bytes 104 | tf_op jit(solution)/shard_map/ppermute | solution.py:33
  19.1 142.2 %collective-permute-start = (bf16[1,1,16,1]{2,3,1,0:T(2,128)(2,1)S(1)}, bf16[1,1,16,1]{2,3,1,0:T(2,128)(2,1)S(1)}, u32[]{:S(2)}, u32[]{:S(2)}) collective-permute-start(bf16[1,1,16,1]{2,3,1,0:T(2,128)(2,1)S(1)} %fusion.82), channel_id=1, source_target_pairs={{3,0},{7,4},{11,8},{15,12},{19,16},{23,20},{27,24},{31,28}} | collective-permute-start | bytes 104 | tf_op jit(solution)/shard_map/ppermute | solution.py:33
  21.4 7.5 %copy-start.6 = (s32[1,2,2,32]{3,2,1,0:T(2,128)S(1)}, s32[1,2,2,32]{3,2,1,0:T(2,128)}, u32[]{:S(2)}) copy-start(s32[1,2,2,32]{3,2,1,0:T(2,128)} %param.12) | copy-start | bytes 1540
  42.5 1.3 copy-start.1
  43.8 34.2 %collective-permute-start.3 = (bf16[1,3,4096]{2,1,0:T(4,128)(2,1)S(1)}, bf16[1,3,4096]{2,1,0:T(4,128)(2,1)S(1)}, u32[]{:S(2)}, u32[]{:S(2)}) collective-permute-start(bf16[1,3,4096]{2,1,0:T(4,128)(2,1)S(1)} %get-tuple-element.18), channel_id=1, source_target_pairs={{0,1},{1,2},{2,3},{4,5},{5,6},{6,7},{8,9},{9,10},{10,11},{12,13},{... | collective-permute-start | bytes 73736 | tf_op jit(solution)/shard_map/ppermute | solution.py:21
  48.4 29.6 %collective-permute-start.4 = (bf16[1,3,4096]{2,1,0:T(4,128)(2,1)S(1)}, bf16[1,3,4096]{2,1,0:T(4,128)(2,1)S(1)}, u32[]{:S(2)}, u32[]{:S(2)}) collective-permute-start(bf16[1,3,4096]{2,1,0:T(4,128)(2,1)S(1)} %get-tuple-element.19), channel_id=1, source_target_pairs={{1,0},{2,1},{3,2},{5,4},{6,5},{7,6},{9,8},{10,9},{11,10},{13,12},{... | collective-permute-start | bytes 73736 | tf_op jit(solution)/shard_map/ppermute | solution.py:23
  62.9 15.1 %copy-start.2 = (bf16[1,256,4096]{2,1,0:T(8,128)(2,1)S(1)}, bf16[1,256,4096]{2,1,0:T(8,128)(2,1)}, u32[]{:S(2)}) copy-start(bf16[1,256,4096]{2,1,0:T(8,128)(2,1)} %copy-done.1) | copy-start | bytes 6291460
  116.9 19.0 %collective-permute-start.9 = (bf16[1,1,16,128,128]{4,3,2,1,0:T(8,128)(2,1)}, bf16[1,1,16,128,128]{4,3,2,1,0:T(8,128)(2,1)S(1)}, u32[]{:S(2)}, u32[]{:S(2)}) collective-permute-start(bf16[1,1,16,128,128]{4,3,2,1,0:T(8,128)(2,1)} %bitcast.69), channel_id=1, source_target_pairs={{1,0},{2,1},{3,2},{5,4},{6,5},{7,6},{9,8},{10,9},{11,10},{13,12},{... | collective-permute-start | bytes 1572872 | tf_op jit(solution)/shard_map/ppermute | solution.py:33
  119.1 21.8 %collective-permute-start.7 = (bf16[1,1,16,128,128]{4,3,2,1,0:T(8,128)(2,1)}, bf16[1,1,16,128,128]{4,3,2,1,0:T(8,128)(2,1)S(1)}, u32[]{:S(2)}, u32[]{:S(2)}) collective-permute-start(bf16[1,1,16,128,128]{4,3,2,1,0:T(8,128)(2,1)} %bitcast.63), channel_id=1, source_target_pairs={{2,0},{3,1},{6,4},{7,5},{10,8},{11,9},{14,12},{15,13},{18,16},{19,... | collective-permute-start | bytes 1572872 | tf_op jit(solution)/shard_map/ppermute | solution.py:33
  126.9 8.9 %copy-start.5 = (bf16[2,8,128,128]{3,2,1,0:T(8,128)(2,1)S(1)}, bf16[2,8,128,128]{3,2,1,0:T(8,128)(2,1)}, u32[]{:S(2)}) copy-start(bf16[2,8,128,128]{3,2,1,0:T(8,128)(2,1)} %copy.39) | copy-start | bytes 1572868
  128.3 20.8 %collective-permute-start.12 = (bf16[1,1,16,1]{2,3,1,0:T(2,128)(2,1)S(1)}, bf16[1,1,16,1]{2,3,1,0:T(2,128)(2,1)S(1)}, u32[]{:S(2)}, u32[]{:S(2)}) collective-permute-start(bf16[1,1,16,1]{2,3,1,0:T(2,128)(2,1)S(1)} %fusion.91), channel_id=1, source_target_pairs={{0,2},{1,3},{4,6},{5,7},{8,10},{9,11},{12,14},{13,15},{16,18},{17,... | collective-permute-start | bytes 104 | tf_op jit(solution)/shard_map/ppermute | solution.py:33
  135.9 14.8 %collective-permute-start.13 = (bf16[1,1,16,128,128]{4,3,2,1,0:T(8,128)(2,1)S(1)}, bf16[1,1,16,128,128]{4,3,2,1,0:T(8,128)(2,1)S(1)}, u32[]{:S(2)}, u32[]{:S(2)}) collective-permute-start(bf16[1,1,16,128,128]{4,3,2,1,0:T(8,128)(2,1)S(1)} %bitcast.249), channel_id=1, source_target_pairs={{0,2},{1,3},{4,6},{5,7},{8,10},{9,11},{12,14},{13,15},{16,18},{17,... | collective-permute-start | bytes 1572872 | tf_op jit(solution)/shard_map/ppermute | solution.py:33
  138.2 2.7 %copy-start.4 = (bf16[2,8,128,128]{3,2,1,0:T(8,128)(2,1)S(1)}, bf16[2,8,128,128]{3,2,1,0:T(8,128)(2,1)}, u32[]{:S(2)}) copy-start(bf16[2,8,128,128]{3,2,1,0:T(8,128)(2,1)} %copy.41) | copy-start | bytes 1572868
  139.0 13.8 %collective-permute-start.14 = (bf16[1,1,16,1]{2,3,1,0:T(2,128)(2,1)S(1)}, bf16[1,1,16,1]{2,3,1,0:T(2,128)(2,1)S(1)}, u32[]{:S(2)}, u32[]{:S(2)}) collective-permute-start(bf16[1,1,16,1]{2,3,1,0:T(2,128)(2,1)S(1)} %fusion.93), channel_id=1, source_target_pairs={{0,3},{4,7},{8,11},{12,15},{16,19},{20,23},{24,27},{28,31}} | collective-permute-start | bytes 104 | tf_op jit(solution)/shard_map/ppermute | solution.py:33
  140.8 19.6 %collective-permute-start.15 = (bf16[1,1,16,128,128]{4,3,2,1,0:T(8,128)(2,1)S(1)}, bf16[1,1,16,128,128]{4,3,2,1,0:T(8,128)(2,1)S(1)}, u32[]{:S(2)}, u32[]{:S(2)}) collective-permute-start(bf16[1,1,16,128,128]{4,3,2,1,0:T(8,128)(2,1)S(1)} %bitcast.248), channel_id=1, source_target_pairs={{0,3},{4,7},{8,11},{12,15},{16,19},{20,23},{24,27},{28,31}} | collective-permute-start | bytes 1572872 | tf_op jit(solution)/shard_map/ppermute | solution.py:33
  148.2 2.4 %copy-start.3 = (bf16[2,8,128,128]{3,2,1,0:T(8,128)(2,1)S(1)}, bf16[2,8,128,128]{3,2,1,0:T(8,128)(2,1)}, u32[]{:S(2)}) copy-start(bf16[2,8,128,128]{3,2,1,0:T(8,128)(2,1)} %copy.31) | copy-start | bytes 1572868
  149.1 19.2 %collective-permute-start.10 = (bf16[1,1,16,1]{2,3,1,0:T(2,128)(2,1)S(1)}, bf16[1,1,16,1]{2,3,1,0:T(2,128)(2,1)S(1)}, u32[]{:S(2)}, u32[]{:S(2)}) collective-permute-start(bf16[1,1,16,1]{2,3,1,0:T(2,128)(2,1)S(1)} %fusion.89), channel_id=1, source_target_pairs={{0,1},{1,2},{2,3},{4,5},{5,6},{6,7},{8,9},{9,10},{10,11},{12,13},{... | collective-permute-start | bytes 104 | tf_op jit(solution)/shard_map/ppermute | solution.py:33
  150.7 16.4 %collective-permute-start.5 = (bf16[1,1,16,128,128]{4,3,2,1,0:T(8,128)(2,1)S(1)}, bf16[1,1,16,128,128]{4,3,2,1,0:T(8,128)(2,1)S(1)}, u32[]{:S(2)}, u32[]{:S(2)}) collective-permute-start(bf16[1,1,16,128,128]{4,3,2,1,0:T(8,128)(2,1)S(1)} %bitcast.247), channel_id=1, source_target_pairs={{3,0},{7,4},{11,8},{15,12},{19,16},{23,20},{27,24},{31,28}} | collective-permute-start | bytes 1572872 | tf_op jit(solution)/shard_map/ppermute | solution.py:33
  152.8 18.0 %collective-permute-start.11 = (bf16[1,1,16,128,128]{4,3,2,1,0:T(8,128)(2,1)S(1)}, bf16[1,1,16,128,128]{4,3,2,1,0:T(8,128)(2,1)S(1)}, u32[]{:S(2)}, u32[]{:S(2)}) collective-permute-start(bf16[1,1,16,128,128]{4,3,2,1,0:T(8,128)(2,1)S(1)} %bitcast.246), channel_id=1, source_target_pairs={{0,1},{1,2},{2,3},{4,5},{5,6},{6,7},{8,9},{9,10},{10,11},{12,13},{... | collective-permute-start | bytes 1572872 | tf_op jit(solution)/shard_map/ppermute | solution.py:33
  160.5 6.6 %copy-start = (f32[64,16384]{1,0:T(8,128)S(1)}, f32[64,16384]{1,0:T(8,128)}, u32[]{:S(2)}) copy-start(f32[64,16384]{1,0:T(8,128)} %fusion.59) | copy-start | bytes 12582916
  174.8 0.7 copy-start.8
Sparse Core Ops, SparseCore 0:
  174.9 51.5 reduce-scatter.2
where the time goes:
time: 239 us; the launch traced here: 235 us
  local copies, waits for them, and re-layouts  57.9 us (24%)
  waiting for transfers between devices  47.4 us (20%)
  starting transfers between devices  41.8 us (17%)
  matrix products  31.8 us (13%)
  other arithmetic  24.1 us (10%)
  blocking collectives  16.3 us (7%)
  between operations  16.1 us (7%)
    reduce_scatter x1, waiting for transfers between devices, local(): lax.psum_scatter(total.reshape(1, CELLS, TILE, TILE), 'visit', scatter_di...  32.8 us
    ppermute x12, starting transfers between devices, passed_along(): return lax.ppermute(x, axis, pairs)  29.8 us
    another operation x2, local copies, waits for them, and re-layouts  27.6 us
    unnamed x1, blocking collectives  16.3 us
    unnamed x31, local copies, waits for them, and re-layouts  16.1 us
    ppermute x12, waiting for transfers between devices, passed_along(): return lax.ppermute(x, axis, pairs)  14.5 us
    concatenate x2, other arithmetic, padded_2(): jnp.concatenate([lax.ppermute(tail, axis, [(i, (i + 1) % count) for i in...  12.2 us
    dot_general x7, matrix products, local(): jnp.dot(chosen, buffer[:, 0].reshape(-1, TILE * TILE), preferred_element_...  9.6 us
  transfers between devices with their start and end apart: 17, of which 4 were waited for; matrix products, arithmetic and copies ran while one was open for 45% of the time, Pallas kernels for 0%

commit v1 on v0

--- a/solution.py
+++ b/solution.py
@@ -1,6 +1,12 @@
+import functools
+
 import jax
 import jax.numpy as jnp
+import ml_dtypes
+import numpy as np
 from jax import lax
+from jax.experimental import pallas as pl
+from jax.experimental.pallas import tpu as pltpu
 from jax.sharding import PartitionSpec as P
 
 TILE = 128
@@ -8,6 +14,13 @@
 SHIFTS = 8
 CELLS = 64
 CAP = 16
+PCELLS = 8
+HALO = 16
+BLOCK = 256
+CORES = 2
+WINDOW = 160
+CHUNK = 2
+MESH = pl.DeviceIdType.MESH
 
 
 def padded_2(cells, sides, width):
@@ -89,7 +102,7 @@
     return chosen.astype(jnp.bfloat16).reshape(classes.shape + table.shape[1:])
 
 
-def local(images, psf_taps, exposure_weights, dest_patch, dest_cell, shift_class):
+def general(images, psf_taps, exposure_weights, dest_patch, dest_cell, shift_class):
     count = images.shape[0]
     band = images.shape[1]
     cols = images.shape[2]
@@ -167,6 +180,329 @@
     return (coadd, cover_sum)
 
 
+def lanczos_windows():
+    out_pos = np.arange(TILE, dtype=np.float64)[None, :, None]
+    src_pos = np.arange(TILE + 6, dtype=np.float64)[None, None, :] - 3.0
+    dist = src_pos - out_pos - np.arange(SHIFTS, dtype=np.float64)[:, None, None] / SHIFTS
+    kernel = np.where(np.abs(dist) < 3.0, np.sinc(dist) * np.sinc(dist / 3.0), 0.0)
+    kernel = kernel / np.sum(kernel, axis=2, keepdims=True)
+    by_cols = np.zeros((SHIFTS, 3 * TILE, TILE), np.float64)
+    by_cols[:, TILE - 3 : 2 * TILE + 3] = kernel.transpose(0, 2, 1)
+    by_rows = np.zeros((SHIFTS, TILE, WINDOW), np.float64)
+    by_rows[:, :, HALO - 3 : HALO + TILE + 3] = kernel
+    return by_cols.astype(ml_dtypes.bfloat16), by_rows.astype(ml_dtypes.bfloat16)
+
+
+def warp_kernel(
+    taps, weight, patch, cell, classes, image, above, below, by_cols, by_rows,
+    tiles, marks, framed, matched, source,
+):
+    band, cols = image.shape
+    height = band + 2 * HALO
+    count_x = cols // TILE
+    slots = tiles.shape[0]
+    reach = KTAPS // 2
+    position = lax.axis_index("patch")
+    last = lax.axis_size("patch") - 1
+
+    def empty(i, carry):
+        source[0, i] = 0
+        source[1, i] = -1
+        return carry
+
+    lax.fori_loop(0, slots, empty, 0)
+
+    def place(i, carry):
+        @pl.when(patch[i] >= 0)
+        def _():
+            row = cell[i] // PCELLS
+            slot = (patch[i] * CORES + row % CORES) * PCELLS + cell[i] % PCELLS
+            source[0, slot] = i
+            source[1, slot] = row // CORES
+
+        return carry
+
+    lax.fori_loop(0, slots, place, 0)
+
+    framed[:, 0:TILE] = jnp.zeros((height, TILE), jnp.bfloat16)
+    framed[:, TILE + cols :] = jnp.zeros((height, TILE), jnp.bfloat16)
+    matched[:, 0:TILE] = jnp.zeros((height, TILE), jnp.bfloat16)
+    matched[:, TILE + cols :] = jnp.zeros((height, TILE), jnp.bfloat16)
+    framed[0:HALO, TILE : TILE + cols] = above[...]
+    framed[HALO : HALO + band, TILE : TILE + cols] = image[...]
+    framed[HALO + band :, TILE : TILE + cols] = below[...]
+
+    shape = (BLOCK + 2 * TILE, BLOCK)
+    lag = (
+        lax.broadcasted_iota(jnp.int32, shape, 0)
+        - lax.broadcasted_iota(jnp.int32, shape, 1)
+        - (TILE - reach)
+    )
+    along = jnp.zeros(shape, jnp.float32)
+    for b in range(KTAPS):
+        along = jnp.where(lag == b, taps[KTAPS + b], along)
+    along = along.astype(jnp.bfloat16)
+    shape = (height, height)
+    out_row = lax.broadcasted_iota(jnp.int32, shape, 0)
+    lag = lax.broadcasted_iota(jnp.int32, shape, 1) - out_row + reach
+    down = jnp.zeros(shape, jnp.float32)
+    for a in range(KTAPS):
+        down = jnp.where(lag == a, taps[a], down)
+    low = jnp.where(position == 0, HALO, 0)
+    high = jnp.where(position == last, HALO + band, height)
+    down = jnp.where((out_row >= low) & (out_row < high), down, 0.0).astype(jnp.bfloat16)
+
+    def match(i, carry):
+        start = pl.multiple_of(i * BLOCK, BLOCK)
+        wide = framed[:, pl.ds(start, BLOCK + 2 * TILE)]
+        passed = jnp.dot(wide, along, preferred_element_type=jnp.float32).astype(jnp.bfloat16)
+        result = jnp.dot(down, passed, preferred_element_type=jnp.float32).astype(jnp.bfloat16)
+        matched[:, pl.ds(pl.multiple_of(start + TILE, TILE), BLOCK)] = result
+        return carry
+
+    lax.fori_loop(0, cols // BLOCK, match, 0, unroll=2)
+
+    def warp(slot, carry):
+        tile = source[0, slot]
+        top = pl.multiple_of(tile // count_x * TILE, TILE)
+        left = pl.multiple_of(tile % count_x * TILE, TILE)
+        window = matched[pl.ds(top, WINDOW), pl.ds(left, 3 * TILE)]
+        half = jnp.dot(
+            window, by_cols[classes[slots + tile]], preferred_element_type=jnp.float32
+        ).astype(jnp.bfloat16)
+        warped = jnp.dot(by_rows[classes[tile]], half, preferred_element_type=jnp.float32)
+        tiles[slot] = warped.astype(jnp.bfloat16)
+        return carry
+
+    lax.fori_loop(0, slots, warp, 0, unroll=4)
+
+    row_of = lax.broadcasted_iota(jnp.int32, (PCELLS, TILE), 0)
+    lane_of = lax.broadcasted_iota(jnp.int32, (PCELLS, TILE), 1)
+
+    def mark(owner, carry):
+        held = jnp.zeros((PCELLS, TILE), jnp.float32)
+        for j in range(PCELLS):
+            here = (row_of == source[1, owner * PCELLS + j]) & (lane_of == j)
+            held = jnp.where(here, weight[0], held)
+        marks[owner] = held
+        return carry
+
+    lax.fori_loop(0, slots // PCELLS, mark, 0)
+
+
+def exchange_kernel(
+    tiles, marks, coadd, cover, got, got_marks, factor, sums, came,
+    tile_out, tile_in, mark_out, mark_in, sum_out, sum_in, own_sem,
+):
+    owners = tiles.shape[0]
+    layers = sums.shape[0]
+    chunks = PCELLS // CHUNK
+    visit = lax.axis_index("visit")
+    patch = lax.axis_index("patch")
+    layer = visit // CORES
+    core = visit % CORES
+    me = patch * CORES + core
+
+    def beside(k):
+        other = lax.rem(me + k, owners)
+        return other, (layer * CORES + other % CORES, other // CORES)
+
+    def along(k):
+        other = lax.rem(layer + k, layers)
+        return other, (other * CORES + core, patch)
+
+    barrier = pltpu.get_barrier_semaphore()
+    for k in range(1, owners):
+        pl.semaphore_signal(barrier, inc=1, device_id=beside(k)[1], device_id_type=MESH)
+    for k in range(1, layers):
+        pl.semaphore_signal(barrier, inc=1, device_id=along(k)[1], device_id_type=MESH)
+    pl.semaphore_wait(barrier, owners + layers - 2)
+
+    def mark_copy(k):
+        other, device = beside(k)
+        return pltpu.make_async_remote_copy(
+            src_ref=marks.at[other], dst_ref=got_marks.at[me],
+            send_sem=mark_out.at[k], recv_sem=mark_in.at[k],
+            device_id=device, device_id_type=MESH,
+        )
+
+    def tile_copy(g, k):
+        other, device = beside(k)
+        part = pl.ds(g * CHUNK, CHUNK)
+        return pltpu.make_async_remote_copy(
+            src_ref=tiles.at[other, part], dst_ref=got.at[me, part],
+            send_sem=tile_out.at[g, k], recv_sem=tile_in.at[g, k],
+            device_id=device, device_id_type=MESH,
+        )
+
+    def sum_copy(g, k):
+        other, device = along(k)
+        part = pl.ds(g * CHUNK, CHUNK)
+        return pltpu.make_async_remote_copy(
+            src_ref=sums.at[other, part], dst_ref=came.at[layer, part],
+            send_sem=sum_out.at[g, k], recv_sem=sum_in.at[g, k],
+            device_id=device, device_id_type=MESH,
+        )
+
+    for k in range(1, owners):
+        mark_copy(k).start()
+    for g in range(chunks):
+        for k in range(1, owners):
+            tile_copy(g, k).start()
+    own = pltpu.make_async_copy(tiles.at[me], got.at[me], own_sem)
+    own.start()
+    got_marks[me] = marks[me]
+    for k in range(1, owners):
+        mark_copy(k).wait_recv()
+    lane_of = lax.broadcasted_iota(jnp.int32, (PCELLS, TILE), 1)
+    for i in range(owners):
+        held = got_marks[i]
+        for j in range(PCELLS):
+            picked = jnp.sum(jnp.where(lane_of == j, held, 0.0), axis=1, keepdims=True)
+            factor[i, j] = jnp.broadcast_to(picked, (PCELLS, TILE))
+    own.wait()
+
+    def terms(row):
+        bands = [b for b in (row - 1, row, row + 1) if 0 <= b < owners // CORES]
+        return [b * CORES + e for b in bands for e in range(CORES)]
+
+    for g in range(chunks):
+        for k in range(1, owners):
+            tile_copy(g, k).wait_recv()
+        for j in range(g * CHUNK, (g + 1) * CHUNK):
+            gain = {
+                (i, row): factor[i, j, row : row + 1, :]
+                for row in range(layers)
+                for i in terms(row)
+            }
+            for row in range(layers):
+                seen = functools.reduce(lambda a, b: a + b, [gain[i, row] for i in terms(row)])
+                sums[row, j, TILE:, :] = jnp.broadcast_to(seen, (PCELLS, TILE))
+
+            def add(n, carry, j=j, gain=gain):
+                rows = pl.ds(pl.multiple_of(n * 16, 16), 16)
+                held = [got[i, j, rows, :].astype(jnp.float32) for i in range(owners)]
+                for row in range(layers):
+                    parts = [gain[i, row] * held[i] for i in terms(row)]
+                    sums[row, j, rows, :] = functools.reduce(lambda a, b: a + b, parts)
+                return carry
+
+            lax.fori_loop(0, TILE // 16, add, 0)
+        for k in range(1, layers):
+            sum_copy(g, k).start()
+    for g in range(chunks):
+        for k in range(1, layers):
+            sum_copy(g, k).wait_recv()
+        for j in range(g * CHUNK, (g + 1) * CHUNK):
+            whole = sums[layer, j]
+            for k in range(1, layers):
+                whole = whole + came[lax.rem(layer + k, layers), j]
+            weight = whole[TILE : TILE + 1, :]
+            coadd[j] = whole[:TILE] / jnp.maximum(weight, 1.0)
+            cover[j : j + 1, :] = weight
+    for k in range(1, owners):
+        mark_copy(k).wait_send()
+        for g in range(chunks):
+            tile_copy(g, k).wait_send()
+    for k in range(1, layers):
+        for g in range(chunks):
+            sum_copy(g, k).wait_send()
+
+
+def whole_rows(images, psf_taps, exposure_weights, dest_patch, dest_cell, shift_class):
+    band, cols = images.shape[1:]
+    bands = lax.axis_size("patch")
+    layers = lax.axis_size("visit") // CORES
+    owners = bands * CORES
+    slots = owners * PCELLS
+    image = images[0]
+    above = lax.ppermute(image[band - HALO :], "patch", [(i, i + 1) for i in range(bands - 1)])
+    below = lax.ppermute(image[:HALO], "patch", [(i + 1, i) for i in range(bands - 1)])
+    by_cols, by_rows = lanczos_windows()
+    scalars = pl.BlockSpec(memory_space=pltpu.SMEM)
+    vector = pl.BlockSpec(memory_space=pltpu.VMEM)
+    height = band + 2 * HALO
+    wide = cols + 2 * TILE
+    tiles, marks = pl.pallas_call(
+        warp_kernel,
+        out_shape=(
+            jax.ShapeDtypeStruct((slots, TILE, TILE), jnp.bfloat16),
+            jax.ShapeDtypeStruct((owners, PCELLS, TILE), jnp.float32),
+        ),
+        in_specs=[scalars] * 5 + [vector] * 5,
+        out_specs=(vector, vector),
+        scratch_shapes=[
+            pltpu.VMEM((height, wide), jnp.bfloat16),
+            pltpu.VMEM((height, wide), jnp.bfloat16),
+            pltpu.SMEM((2, slots), jnp.int32),
+        ],
+        compiler_params=pltpu.CompilerParams(vmem_limit_bytes=40 * 2**20),
+        cost_estimate=pl.CostEstimate(
+            flops=3 * 10**9, bytes_accessed=6 * 2**20, transcendentals=0
+        ),
+        name="match_and_warp",
+    )(
+        psf_taps.astype(jnp.float32).reshape(-1),
+        exposure_weights,
+        dest_patch.reshape(-1),
+        dest_cell.reshape(-1),
+        shift_class.reshape(-1),
+        image,
+        above,
+        below,
+        jnp.asarray(by_cols),
+        jnp.asarray(by_rows),
+    )
+    chunks = PCELLS // CHUNK
+    dma = pltpu.SemaphoreType.DMA
+    coadd, cover = pl.pallas_call(
+        exchange_kernel,
+        out_shape=(
+            jax.ShapeDtypeStruct((PCELLS, TILE, TILE), jnp.float32),
+            jax.ShapeDtypeStruct((PCELLS, TILE), jnp.float32),
+        ),
+        in_specs=[vector, vector],
+        out_specs=(vector, vector),
+        scratch_shapes=[
+            pltpu.VMEM((owners, PCELLS, TILE, TILE), jnp.bfloat16),
+            pltpu.VMEM((owners, PCELLS, TILE), jnp.float32),
+            pltpu.VMEM((owners, PCELLS, PCELLS, TILE), jnp.float32),
+            pltpu.VMEM((layers, PCELLS, TILE + PCELLS, TILE), jnp.float32),
+            pltpu.VMEM((layers, PCELLS, TILE + PCELLS, TILE), jnp.float32),
+            dma((chunks, owners)),
+            dma((chunks, owners)),
+            dma((owners,)),
+            dma((owners,)),
+            dma((chunks, layers)),
+            dma((chunks, layers)),
+            dma,
+        ],
+        compiler_params=pltpu.CompilerParams(
+            collective_id=0, has_side_effects=True, vmem_limit_bytes=40 * 2**20
+        ),
+        cost_estimate=pl.CostEstimate(
+            flops=10**8, bytes_accessed=6 * 2**20, transcendentals=0
+        ),
+        name="exchange_and_sum",
+    )(tiles.reshape(owners, PCELLS, TILE, TILE), marks)
+    return coadd[None], cover[:, 0][None]
+
+
+def local(images, psf_taps, exposure_weights, dest_patch, dest_cell, shift_class):
+    count, band, cols = images.shape
+    owners = lax.axis_size("patch")
+    visits = lax.axis_size("visit")
+    row_of_patches = (
+        count == 1
+        and band == CORES * TILE
+        and owners * band == PCELLS * TILE
+        and cols == owners * PCELLS * TILE
+        and visits == PCELLS
+    )
+    plan = whole_rows if row_of_patches else general
+    return plan(images, psf_taps, exposure_weights, dest_patch, dest_cell, shift_class)
+
+
 def solution(mesh):
     placed = (
         P("visit", "patch", None),

time: 239 us -> 103 us (0.43)
  the two profiles are of different devices: /device:TPU:0 before, /device:TPU:11 now
where the time goes in v1:
time: 103 us
  Pallas kernels  86.4 us (84%)
  local copies, waits for them, and re-layouts  9.18 us (9%)
  starting transfers between devices  6.18 us (6%)
  between operations  1.33 us (1%)
    pallas_call x1, Pallas kernels, whole_rows(): pl.pallas_call(exchange_kernel, out_shape=(jax.ShapeDtypeStruct((PCELLS,...  63.2 us
    pallas_call x1, Pallas kernels, whole_rows(): pl.pallas_call(warp_kernel, out_shape=(jax.ShapeDtypeStruct((slots, TILE,...  23.2 us
    unnamed x7, local copies, waits for them, and re-layouts  4.55 us
    ppermute x1, starting transfers between devices, whole_rows(): lax.ppermute(image[band - HALO:], 'patch', [(i, i + 1) for i in range(ban...  4.02 us
    ppermute x1, starting transfers between devices, whole_rows(): lax.ppermute(image[:HALO], 'patch', [(i + 1, i) for i in range(bands - 1)])  2.16 us
  transfers between devices with their start and end apart: 2, of which 0 were waited for; matrix products, arithmetic and copies ran while one was open for 3% of the time, Pallas kernels for 0%

profile of v1, /device:TPU:11, one launch (start us, length us, event | category | flops | bytes accessed | tf_op | source)
XLA Modules:
  0.0 103.1 jit_solution(12939076780576407557)
XLA Ops:
  0.6 1.0 slice_bitcast_fusion
  1.6 2.2 %collective-permute-start.1 = (bf16[16,4096]{1,0:T(8,128)(2,1)S(1)}, bf16[16,4096]{1,0:T(8,128)(2,1)S(1)}, u32[]{:S(2)}, u32[]{:S(2)}) collective-permute-start(bf16[16,4096]{1,0:T(8,128)(2,1)S(1)} %get-tuple-element.10), channel_id=1, source_target_pairs={{1,0},{2,1},{3,2},{5,4},{6,5},{7,6},{9,8},{10,9},{11,10},{13,12},{... | collective-permute-start | bytes 393224 | tf_op jit(solution)/shard_map/ppermute | solution.py:420
  3.8 4.0 %collective-permute-start = (bf16[16,4096]{1,0:T(8,128)(2,1)S(1)}, bf16[16,4096]{1,0:T(8,128)(2,1)S(1)}, u32[]{:S(2)}, u32[]{:S(2)}) collective-permute-start(bf16[16,4096]{1,0:T(8,128)(2,1)S(1)} %get-tuple-element.11), channel_id=1, source_target_pairs={{0,1},{1,2},{2,3},{4,5},{5,6},{6,7},{8,9},{9,10},{10,11},{12,13},{... | collective-permute-start | bytes 393224 | tf_op jit(solution)/shard_map/ppermute | solution.py:419
  8.5 0.7 reshape.30.taps
  9.2 0.8 reshape.25.patch
  10.0 0.8 reshape.26.cell
  10.7 0.8 reshape.27.classes
  11.5 0.0 collective-permute-done.1.below
  11.5 0.0 collective-permute-done.above
  11.5 0.0 copy-start
  11.5 1.6 %copy-done = bf16[1,256,4096]{2,1,0:T(8,128)(2,1)S(1)} copy-done((bf16[1,256,4096]{2,1,0:T(8,128)(2,1)S(1)}, bf16[1,256,4096]{2,1,0:T(8,128)(2,1)}, u32[]{:S(2)}) %copy-start) | copy-done | bytes 2097176
  13.1 0.0 copy-start.1
  13.1 1.1 %copy-done.1 = bf16[8,384,128]{2,1,0:T(8,128)(2,1)S(1)} copy-done((bf16[8,384,128]{2,1,0:T(8,128)(2,1)S(1)}, bf16[8,384,128]{2,1,0:T(8,128)(2,1)}, u32[]{:S(2)}) %copy-start.1) | copy-done | bytes 786456
  14.2 0.0 copy-start.2
  14.2 1.0 %copy-done.2 = bf16[8,128,160]{2,1,0:T(8,128)(2,1)S(1)} copy-done((bf16[8,128,160]{2,1,0:T(8,128)(2,1)S(1)}, bf16[8,128,160]{2,1,0:T(8,128)(2,1)}, u32[]{:S(2)}) %copy-start.2) | copy-done | bytes 327704
  15.3 23.2 %match_and_warp.1 = (bf16[64,128,128]{2,1,0:T(8,128)(2,1)S(1)}, f32[8,8,128]{2,1,0:T(8,128)S(1)}) custom-call(f32[26]{0:T(128)S(1)} %reshape.30.taps, f32[1]{0:T(128)S(6)} %copy.11.weight, s32[64]{0:T(128)S(1)} %reshape.25.patch, s32[64]{0:T(128)S(1)} %reshape.26.cell, s32[128]{0:T(128)S(1)} %reshape.27.classes, bf16[256,4096]{1,0:T(8,128)(2,1)S(1)} %bitcast.10, ...), custom_call_target="tpu_custom_call" | custom-call | flops 3000000000 | bytes 6291456 | tf_op jit(solution)/shard_map/match_and_warp/pallas_call | solution.py:426
  38.5 63.2 %exchange_and_sum.1 = (f32[8,128,128]{2,1,0:T(8,128)S(1)}, f32[8,128]{1,0:T(8,128)S(1)}) custom-call(bf16[8,8,128,128]{3,2,1,0:T(8,128)(2,1)S(1)} %bitcast.8, f32[8,8,128]{2,1,0:T(8,128)S(1)} %get-tuple-element.7.marks), custom_call_target="tpu_custom_call" | custom-call | flops 100000000 | bytes 6291456 | tf_op jit(solution)/shard_map/exchange_and_sum/pallas_call | solution.py:458
  101.7 0.6 slice_reduce_fusion
  102.3 0.8 copy.12
Async XLA Ops:
  1.6 9.9 %collective-permute-start.1 = (bf16[16,4096]{1,0:T(8,128)(2,1)S(1)}, bf16[16,4096]{1,0:T(8,128)(2,1)S(1)}, u32[]{:S(2)}, u32[]{:S(2)}) collective-permute-start(bf16[16,4096]{1,0:T(8,128)(2,1)S(1)} %get-tuple-element.10), channel_id=1, source_target_pairs={{1,0},{2,1},{3,2},{5,4},{6,5},{7,6},{9,8},{10,9},{11,10},{13,12},{... | collective-permute-start | bytes 393224 | tf_op jit(solution)/shard_map/ppermute | solution.py:420
  3.8 7.7 %collective-permute-start = (bf16[16,4096]{1,0:T(8,128)(2,1)S(1)}, bf16[16,4096]{1,0:T(8,128)(2,1)S(1)}, u32[]{:S(2)}, u32[]{:S(2)}) collective-permute-start(bf16[16,4096]{1,0:T(8,128)(2,1)S(1)} %get-tuple-element.11), channel_id=1, source_target_pairs={{0,1},{1,2},{2,3},{4,5},{5,6},{6,7},{8,9},{9,10},{10,11},{12,13},{... | collective-permute-start | bytes 393224 | tf_op jit(solution)/shard_map/ppermute | solution.py:419
  11.5 1.6 %copy-start = (bf16[1,256,4096]{2,1,0:T(8,128)(2,1)S(1)}, bf16[1,256,4096]{2,1,0:T(8,128)(2,1)}, u32[]{:S(2)}) copy-start(bf16[1,256,4096]{2,1,0:T(8,128)(2,1)} %param.8) | copy-start | bytes 6291460
  13.1 1.1 %copy-start.1 = (bf16[8,384,128]{2,1,0:T(8,128)(2,1)S(1)}, bf16[8,384,128]{2,1,0:T(8,128)(2,1)}, u32[]{:S(2)}) copy-start(bf16[8,384,128]{2,1,0:T(8,128)(2,1)} %constant.4.clone.by_cols) | copy-start | bytes 2359300
  14.2 1.0 %copy-start.2 = (bf16[8,128,160]{2,1,0:T(8,128)(2,1)S(1)}, bf16[8,128,160]{2,1,0:T(8,128)(2,1)}, u32[]{:S(2)}) copy-start(bf16[8,128,160]{2,1,0:T(8,128)(2,1)} %constant.5.clone.by_rows) | copy-start | bytes 983044

commit v2 on v1

--- a/solution.py
+++ b/solution.py
@@ -18,7 +18,8 @@
 HALO = 16
 BLOCK = 256
 CORES = 2
-WINDOW = 160
+WINDOW = 144
+EDGE = 3
 CHUNK = 2
 MESH = pl.DeviceIdType.MESH
 
@@ -186,24 +187,36 @@
     dist = src_pos - out_pos - np.arange(SHIFTS, dtype=np.float64)[:, None, None] / SHIFTS
     kernel = np.where(np.abs(dist) < 3.0, np.sinc(dist) * np.sinc(dist / 3.0), 0.0)
     kernel = kernel / np.sum(kernel, axis=2, keepdims=True)
-    by_cols = np.zeros((SHIFTS, 3 * TILE, TILE), np.float64)
-    by_cols[:, TILE - 3 : 2 * TILE + 3] = kernel.transpose(0, 2, 1)
+    by_cols = np.zeros((SHIFTS, 2 * TILE, TILE), np.float64)
+    by_cols[:, : TILE + 2 * EDGE] = kernel.transpose(0, 2, 1)
     by_rows = np.zeros((SHIFTS, TILE, WINDOW), np.float64)
-    by_rows[:, :, HALO - 3 : HALO + TILE + 3] = kernel
+    by_rows[:, :, : TILE + 2 * EDGE] = kernel
     return by_cols.astype(ml_dtypes.bfloat16), by_rows.astype(ml_dtypes.bfloat16)
 
 
 def warp_kernel(
-    taps, weight, patch, cell, classes, image, above, below, by_cols, by_rows,
-    tiles, marks, framed, matched, source,
+    patches, cells, classes, weight, taps, image, above, below, table_cols, table_rows,
+    tiles, marks, framed, matched, by_cols, by_rows, source, sems,
 ):
-    band, cols = image.shape
+    band, cols = image.shape[1:]
+    count_x = cols // TILE
     height = band + 2 * HALO
-    count_x = cols // TILE
+    reach = KTAPS // 2
     slots = tiles.shape[0]
-    reach = KTAPS // 2
-    position = lax.axis_index("patch")
+    patch = lax.axis_index("patch")
     last = lax.axis_size("patch") - 1
+
+    framed[:, 0:TILE] = jnp.zeros((height, TILE), jnp.bfloat16)
+    framed[:, TILE + cols :] = jnp.zeros((height, framed.shape[1] - TILE - cols), jnp.bfloat16)
+    pieces = ((image.at[0], HALO, band), (above, 0, HALO), (below, HALO + band, HALO))
+    loads = [
+        pltpu.make_async_copy(ref, framed.at[pl.ds(top, rows), pl.ds(TILE, cols)], sems.at[i])
+        for i, (ref, top, rows) in enumerate(pieces)
+    ]
+    load_cols = pltpu.make_async_copy(table_cols, by_cols, sems.at[3])
+    load_rows = pltpu.make_async_copy(table_rows, by_rows, sems.at[4])
+    for load in loads + [load_cols, load_rows]:
+        load.start()
 
     def empty(i, carry):
         source[0, i] = 0
@@ -213,10 +226,14 @@
     lax.fori_loop(0, slots, empty, 0)
 
     def place(i, carry):
-        @pl.when(patch[i] >= 0)
+        y, x = i // count_x, i % count_x
+        owner = patches[0, y, x]
+
+        @pl.when(owner >= 0)
         def _():
-            row = cell[i] // PCELLS
-            slot = (patch[i] * CORES + row % CORES) * PCELLS + cell[i] % PCELLS
+            cell = cells[0, y, x]
+            row = cell // PCELLS
+            slot = (owner * CORES + row % CORES) * PCELLS + cell % PCELLS
             source[0, slot] = i
             source[1, slot] = row // CORES
 
@@ -224,57 +241,73 @@
 
     lax.fori_loop(0, slots, place, 0)
 
-    framed[:, 0:TILE] = jnp.zeros((height, TILE), jnp.bfloat16)
-    framed[:, TILE + cols :] = jnp.zeros((height, TILE), jnp.bfloat16)
-    matched[:, 0:TILE] = jnp.zeros((height, TILE), jnp.bfloat16)
-    matched[:, TILE + cols :] = jnp.zeros((height, TILE), jnp.bfloat16)
-    framed[0:HALO, TILE : TILE + cols] = above[...]
-    framed[HALO : HALO + band, TILE : TILE + cols] = image[...]
-    framed[HALO + band :, TILE : TILE + cols] = below[...]
-
+    tap = taps[0].astype(jnp.float32)
     shape = (BLOCK + 2 * TILE, BLOCK)
     lag = (
         lax.broadcasted_iota(jnp.int32, shape, 0)
         - lax.broadcasted_iota(jnp.int32, shape, 1)
-        - (TILE - reach)
+        - (TILE - reach - EDGE)
     )
-    along = jnp.zeros(shape, jnp.float32)
+    across = jnp.zeros(shape, jnp.float32)
     for b in range(KTAPS):
-        along = jnp.where(lag == b, taps[KTAPS + b], along)
-    along = along.astype(jnp.bfloat16)
-    shape = (height, height)
-    out_row = lax.broadcasted_iota(jnp.int32, shape, 0)
-    lag = lax.broadcasted_iota(jnp.int32, shape, 1) - out_row + reach
+        across = jnp.where(lag == b, tap[1:2, b : b + 1], across)
+    across = across.astype(jnp.bfloat16)
+    shape = (matched.shape[0], height)
+    frame_row = lax.broadcasted_iota(jnp.int32, shape, 0) + (HALO - EDGE)
+    lag = lax.broadcasted_iota(jnp.int32, shape, 1) - frame_row + reach
     down = jnp.zeros(shape, jnp.float32)
     for a in range(KTAPS):
-        down = jnp.where(lag == a, taps[a], down)
-    low = jnp.where(position == 0, HALO, 0)
-    high = jnp.where(position == last, HALO + band, height)
-    down = jnp.where((out_row >= low) & (out_row < high), down, 0.0).astype(jnp.bfloat16)
+        down = jnp.where(lag == a, tap[0:1, a : a + 1], down)
+    low = jnp.where(patch == 0, HALO, 0)
+    high = jnp.where(patch == last, HALO + band, height)
+    down = jnp.where((frame_row >= low) & (frame_row < high), down, 0.0).astype(jnp.bfloat16)
+
+    for load in loads:
+        load.wait()
 
     def match(i, carry):
         start = pl.multiple_of(i * BLOCK, BLOCK)
         wide = framed[:, pl.ds(start, BLOCK + 2 * TILE)]
-        passed = jnp.dot(wide, along, preferred_element_type=jnp.float32).astype(jnp.bfloat16)
+        passed = jnp.dot(wide, across, preferred_element_type=jnp.float32).astype(jnp.bfloat16)
         result = jnp.dot(down, passed, preferred_element_type=jnp.float32).astype(jnp.bfloat16)
-        matched[:, pl.ds(pl.multiple_of(start + TILE, TILE), BLOCK)] = result
+        matched[:, pl.ds(start, BLOCK)] = result
         return carry
 
-    lax.fori_loop(0, cols // BLOCK, match, 0, unroll=2)
-
-    def warp(slot, carry):
-        tile = source[0, slot]
-        top = pl.multiple_of(tile // count_x * TILE, TILE)
-        left = pl.multiple_of(tile % count_x * TILE, TILE)
-        window = matched[pl.ds(top, WINDOW), pl.ds(left, 3 * TILE)]
-        half = jnp.dot(
-            window, by_cols[classes[slots + tile]], preferred_element_type=jnp.float32
-        ).astype(jnp.bfloat16)
-        warped = jnp.dot(by_rows[classes[tile]], half, preferred_element_type=jnp.float32)
-        tiles[slot] = warped.astype(jnp.bfloat16)
+    lax.fori_loop(0, cols // BLOCK, match, 0, unroll=4)
+    wide = framed[:, cols : cols + 3 * TILE]
+    passed = jnp.dot(
+        wide, across[: 3 * TILE, :TILE], preferred_element_type=jnp.float32
+    ).astype(jnp.bfloat16)
+    result = jnp.dot(down, passed, preferred_element_type=jnp.float32)
+    lane = lax.broadcasted_iota(jnp.int32, result.shape, 1)
+    matched[:, cols:] = jnp.where(lane < EDGE, result, 0.0).astype(jnp.bfloat16)
+    begin = matched[:, 0:TILE].astype(jnp.float32)
+    matched[:, 0:TILE] = jnp.where(lane < EDGE, 0.0, begin).astype(jnp.bfloat16)
+    load_cols.wait()
+    load_rows.wait()
+
+    def warp(n, carry):
+        todo = [n * PCELLS + j for j in range(PCELLS)]
+        places = [(source[0, t] // count_x, source[0, t] % count_x) for t in todo]
+        halves = []
+        for y, x in places:
+            top = pl.multiple_of(y * TILE, TILE)
+            left = pl.multiple_of(x * TILE, TILE)
+            window = matched[pl.ds(top, WINDOW), pl.ds(left, 2 * TILE)]
+            halves.append(
+                jnp.dot(
+                    window, by_cols[classes[0, 1, y, x]], preferred_element_type=jnp.float32
+                ).astype(jnp.bfloat16)
+            )
+        warped = [
+            jnp.dot(by_rows[classes[0, 0, y, x]], half, preferred_element_type=jnp.float32)
+            for (y, x), half in zip(places, halves)
+        ]
+        for t, block in zip(todo, warped):
+            tiles[t] = block.astype(jnp.bfloat16)
         return carry
 
-    lax.fori_loop(0, slots, warp, 0, unroll=4)
+    lax.fori_loop(0, slots // PCELLS, warp, 0)
 
     row_of = lax.broadcasted_iota(jnp.int32, (PCELLS, TILE), 0)
     lane_of = lax.broadcasted_iota(jnp.int32, (PCELLS, TILE), 1)
@@ -346,7 +379,7 @@
 
     for k in range(1, owners):
         mark_copy(k).start()
-    for g in range(chunks):
+    for g in range(2):
         for k in range(1, owners):
             tile_copy(g, k).start()
     own = pltpu.make_async_copy(tiles.at[me], got.at[me], own_sem)
@@ -369,6 +402,9 @@
     for g in range(chunks):
         for k in range(1, owners):
             tile_copy(g, k).wait_recv()
+        if g + 2 < chunks:
+            for k in range(1, owners):
+                tile_copy(g + 2, k).start()
         for j in range(g * CHUNK, (g + 1) * CHUNK):
             gain = {
                 (i, row): factor[i, j, row : row + 1, :]
@@ -422,32 +458,35 @@
     scalars = pl.BlockSpec(memory_space=pltpu.SMEM)
     vector = pl.BlockSpec(memory_space=pltpu.VMEM)
     height = band + 2 * HALO
-    wide = cols + 2 * TILE
+    anywhere = pl.BlockSpec(memory_space=pl.ANY)
     tiles, marks = pl.pallas_call(
         warp_kernel,
         out_shape=(
             jax.ShapeDtypeStruct((slots, TILE, TILE), jnp.bfloat16),
             jax.ShapeDtypeStruct((owners, PCELLS, TILE), jnp.float32),
         ),
-        in_specs=[scalars] * 5 + [vector] * 5,
+        in_specs=[scalars] * 4 + [vector] + [anywhere] * 5,
         out_specs=(vector, vector),
         scratch_shapes=[
-            pltpu.VMEM((height, wide), jnp.bfloat16),
-            pltpu.VMEM((height, wide), jnp.bfloat16),
+            pltpu.VMEM((height, cols + 3 * TILE), jnp.bfloat16),
+            pltpu.VMEM((band + HALO, cols + TILE), jnp.bfloat16),
+            pltpu.VMEM(by_cols.shape, jnp.bfloat16),
+            pltpu.VMEM(by_rows.shape, jnp.bfloat16),
             pltpu.SMEM((2, slots), jnp.int32),
+            pltpu.SemaphoreType.DMA((5,)),
         ],
-        compiler_params=pltpu.CompilerParams(vmem_limit_bytes=40 * 2**20),
+        compiler_params=pltpu.CompilerParams(vmem_limit_bytes=60 * 2**20),
         cost_estimate=pl.CostEstimate(
             flops=3 * 10**9, bytes_accessed=6 * 2**20, transcendentals=0
         ),
         name="match_and_warp",
     )(
-        psf_taps.astype(jnp.float32).reshape(-1),
+        dest_patch,
+        dest_cell,
+        shift_class,
         exposure_weights,
-        dest_patch.reshape(-1),
-        dest_cell.reshape(-1),
-        shift_class.reshape(-1),
-        image,
+        psf_taps,
+        images,
         above,
         below,
         jnp.asarray(by_cols),

time: 103 us -> 96.8 us (0.940)
  Pallas kernels: 86.4 us -> 82.3 us
  local copies, waits for them, and re-layouts: 9.18 us -> 5.41 us
  waiting for transfers between devices: 0.01 us -> 1.33 us
    pallas_call x1, Pallas kernels: 23.2 us -> 17.6 us  [whole_rows(): pl.pallas_call(warp_kernel, out_shape=(jax.ShapeDtypeStruct((slots, TILE,...]
    reshape x4 -> x0, local copies, waits for them, and re-layouts: 3.02 us -> none  [the longest x1 0.76 us: whole_rows(): shift_class.reshape(-1)]
    pallas_call x1, Pallas kernels: 63.2 us -> 64.7 us  [whole_rows(): pl.pallas_call(exchange_kernel, out_shape=(jax.ShapeDtypeStruct((PCELLS,...]
    unnamed x7 -> x9, local copies, waits for them, and re-layouts: 4.55 us -> 3.79 us
  transfers between devices with their start and end apart: 2 -> 2, of which waited for: 0 -> 2; matrix products, arithmetic and copies ran while one was open for 3% -> 0% of each run, Pallas kernels for 0% -> 0%
where the time goes in v2:
time: 96.8 us; the launch traced here: 96.5 us
  Pallas kernels  82.3 us (85%)
  starting transfers between devices  6.18 us (6%)
  local copies, waits for them, and re-layouts  5.41 us (6%)
  waiting for transfers between devices  1.33 us (1%)
  between operations  1.32 us (1%)
    pallas_call x1, Pallas kernels, whole_rows(): pl.pallas_call(exchange_kernel, out_shape=(jax.ShapeDtypeStruct((PCELLS,...  64.7 us
    pallas_call x1, Pallas kernels, whole_rows(): pl.pallas_call(warp_kernel, out_shape=(jax.ShapeDtypeStruct((slots, TILE,...  17.6 us
    ppermute x1, starting transfers between devices, whole_rows(): lax.ppermute(image[band - HALO:], 'patch', [(i, i + 1) for i in range(ban...  4.02 us
    unnamed x9, local copies, waits for them, and re-layouts  3.79 us
    ppermute x1, starting transfers between devices, whole_rows(): lax.ppermute(image[:HALO], 'patch', [(i + 1, i) for i in range(bands - 1)])  2.16 us
  transfers between devices with their start and end apart: 2, of which 2 were waited for; matrix products, arithmetic and copies ran while one was open for 0% of the time, Pallas kernels for 0%

profile of v2, /device:TPU:11, one launch (start us, length us, event | category | flops | bytes accessed | tf_op | source)
XLA Modules:
  0.0 96.5 jit_solution(2642884133079575240)
XLA Ops:
  0.6 1.0 %slice_bitcast_fusion = (bf16[16,4096]{1,0:T(8,128)(2,1)S(1)}, bf16[16,4096]{1,0:T(8,128)(2,1)S(1)}) fusion(bf16[1,256,4096]{2,1,0:T(8,128)(2,1)} %image.1), kind=kLoop, calls=%fused_computation | loop fusion | bytes 524288 | tf_op jit(solution)/shard_map/slice | solution.py:456
  1.6 2.2 %collective-permute-start.1 = (bf16[16,4096]{1,0:T(8,128)(2,1)S(1)}, bf16[16,4096]{1,0:T(8,128)(2,1)S(1)}, u32[]{:S(2)}, u32[]{:S(2)}) collective-permute-start(bf16[16,4096]{1,0:T(8,128)(2,1)S(1)} %get-tuple-element.10), channel_id=1, source_target_pairs={{1,0},{2,1},{3,2},{5,4},{6,5},{7,6},{9,8},{10,9},{11,10},{13,12},{... | collective-permute-start | bytes 393224 | tf_op jit(solution)/shard_map/ppermute | solution.py:456
  3.8 4.0 %collective-permute-start = (bf16[16,4096]{1,0:T(8,128)(2,1)S(1)}, bf16[16,4096]{1,0:T(8,128)(2,1)S(1)}, u32[]{:S(2)}, u32[]{:S(2)}) collective-permute-start(bf16[16,4096]{1,0:T(8,128)(2,1)S(1)} %get-tuple-element.11), channel_id=1, source_target_pairs={{0,1},{1,2},{2,3},{4,5},{5,6},{6,7},{8,9},{9,10},{10,11},{12,13},{... | collective-permute-start | bytes 393224 | tf_op jit(solution)/shard_map/ppermute | solution.py:455
  8.5 0.3 collective-permute-done.1.below
  8.8 0.0 copy-start.2
  8.8 1.0 %collective-permute-done.above = bf16[16,4096]{1,0:T(8,128)(2,1)S(1)} collective-permute-done((bf16[16,4096]{1,0:T(8,128)(2,1)S(1)}, bf16[16,4096]{1,0:T(8,128)(2,1)S(1)}, u32[]{:S(2)}, u32[]{:S(2)}) %collective-permute-start) | collective-permute-done | bytes 131104 | tf_op jit(solution)/shard_map/ppermute | solution.py:455
  9.8 0.0 copy-done.2
  9.8 0.0 copy-start.3
  9.8 0.7 copy-done.3
  10.5 17.6 %match_and_warp.1 = (bf16[64,128,128]{2,1,0:T(8,128)(2,1)}, f32[8,8,128]{2,1,0:T(8,128)}) custom-call(s32[1,2,32]{2,1,0:T(2,128)} %patches.1, s32[1,2,32]{2,1,0:T(2,128)} %cells.1, s32[1,2,2,32]{3,2,1,0:T(2,128)} %classes.1, f32[1]{0:T(128)S(6)} %copy.11.weight, bf16[1,2,13]{2,1,0:T(2,128)(2,1)} %taps.1, bf16[1,256,4096]{2,1,0:T(8,128)(2,1)} %image.1, ...), custom_call_target="tpu_custom_call" | custom-call | flops 3000000000 | bytes 6291456 | tf_op jit(solution)/shard_map/match_and_warp/pallas_call | solution.py:462
  28.1 0.0 copy-start
  28.1 1.6 %copy-done = bf16[64,128,128]{2,1,0:T(8,128)(2,1)S(1)} copy-done((bf16[64,128,128]{2,1,0:T(8,128)(2,1)S(1)}, bf16[64,128,128]{2,1,0:T(8,128)(2,1)}, u32[]{:S(2)}) %copy-start) | copy-done | bytes 2097176
  29.7 0.0 copy-start.1
  29.7 0.8 copy-done.1
  30.4 64.7 %exchange_and_sum.1 = (f32[8,128,128]{2,1,0:T(8,128)S(1)}, f32[8,128]{1,0:T(8,128)S(1)}) custom-call(bf16[8,8,128,128]{3,2,1,0:T(8,128)(2,1)S(1)} %bitcast.7, f32[8,8,128]{2,1,0:T(8,128)S(1)} %copy-done.1), custom_call_target="tpu_custom_call" | custom-call | flops 100000000 | bytes 6291456 | tf_op jit(solution)/shard_map/exchange_and_sum/pallas_call | solution.py:497
  95.1 0.6 slice_reduce_fusion
  95.7 0.8 copy.12
Async XLA Ops:
  1.6 7.2 %collective-permute-start.1 = (bf16[16,4096]{1,0:T(8,128)(2,1)S(1)}, bf16[16,4096]{1,0:T(8,128)(2,1)S(1)}, u32[]{:S(2)}, u32[]{:S(2)}) collective-permute-start(bf16[16,4096]{1,0:T(8,128)(2,1)S(1)} %get-tuple-element.10), channel_id=1, source_target_pairs={{1,0},{2,1},{3,2},{5,4},{6,5},{7,6},{9,8},{10,9},{11,10},{13,12},{... | collective-permute-start | bytes 393224 | tf_op jit(solution)/shard_map/ppermute | solution.py:456
  3.8 6.0 %collective-permute-start = (bf16[16,4096]{1,0:T(8,128)(2,1)S(1)}, bf16[16,4096]{1,0:T(8,128)(2,1)S(1)}, u32[]{:S(2)}, u32[]{:S(2)}) collective-permute-start(bf16[16,4096]{1,0:T(8,128)(2,1)S(1)} %get-tuple-element.11), channel_id=1, source_target_pairs={{0,1},{1,2},{2,3},{4,5},{5,6},{6,7},{8,9},{9,10},{10,11},{12,13},{... | collective-permute-start | bytes 393224 | tf_op jit(solution)/shard_map/ppermute | solution.py:455
  8.8 1.0 %copy-start.2 = (bf16[16,4096]{1,0:T(8,128)(2,1)}, bf16[16,4096]{1,0:T(8,128)(2,1)S(1)}, u32[]{:S(2)}) copy-start(bf16[16,4096]{1,0:T(8,128)(2,1)S(1)} %collective-permute-done.1.below) | copy-start | bytes 393220
  9.8 0.7 copy-start.3
  28.1 1.6 %copy-start = (bf16[64,128,128]{2,1,0:T(8,128)(2,1)S(1)}, bf16[64,128,128]{2,1,0:T(8,128)(2,1)}, u32[]{:S(2)}) copy-start(bf16[64,128,128]{2,1,0:T(8,128)(2,1)} %get-tuple-element.6) | copy-start | bytes 6291460
  29.7 0.8 copy-start.1
